TPU v7x, 32 devices: a whole 2x2x4 slice. The times are simulated.
32 devices in a mesh: shots: 2 (over x), gx: 16 (over z, y, core).
Axes of the slice: x: 2, y: 2, z: 4, core: 2. Of those that a mesh axis runs over, the one named last changes fastest.
Arguments:
- displacement: float32 [3, 256, 256, 128], P(None, ('shots', 'gx')), parts along dimension 1, may hold values from -9 to 9
- adjoint: float32 [3, 256, 256, 128], P(None, ('shots', 'gx')), parts along dimension 1, may hold values from -6 to 6
- vp_model: float32 [256, 256, 128], P(('shots', 'gx')), parts along dimension 0, may hold values from 1.5 to 6
- vs_model: float32 [256, 256, 128], P(('shots', 'gx')), parts along dimension 0, may hold values from 0.8 to 3.5
Outputs:
- kernel_p: float32 [256, 256, 128], P(('shots', 'gx')), parts along dimension 0
- kernel_s: float32 [256, 256, 128], P(('shots', 'gx')), parts along dimension 0
There are 2 independent parts, one for each index of `shots`. A program takes and returns all parts, laid end to end along the dimension named above; each array names one. Nothing has to cross between parts.
All inputs are finite; a program needn't handle non-finite values.
Results may differ from a plain program's by a relative error of at most 0.0001.
Values sent between devices are 32-bit elements; how exact they have to be, the bound alone decides.
A program may use at most 64 MiB of HBM per device.

v0:
```python
import jax
import jax.numpy as jnp
from jax import lax
from jax.sharding import PartitionSpec as P

ITERS = 3


def extended(block, sides, width):
    for axis, dim in sides:
        count = lax.axis_size(axis)
        forward = [(i, i + 1) for i in range(count - 1)]
        backward = [(target, source) for source, target in forward]
        low = lax.ppermute(
            lax.slice_in_dim(block, block.shape[dim] - width, None, axis=dim), axis, forward
        )
        high = lax.ppermute(lax.slice_in_dim(block, 0, width, axis=dim), axis, backward)
        block = jnp.concatenate([low, block, high], axis=dim)
    return block


def derive(padded_x):
    along_x = (padded_x[:, 2:] - padded_x[:, :-2]) / 2.0
    core = padded_x[:, 1:-1]
    padded = jnp.pad(core, ((0, 0), (0, 0), (1, 1), (1, 1)))
    along_y = (padded[:, :, 2:, 1:-1] - padded[:, :, :-2, 1:-1]) / 2.0
    along_z = (padded[:, :, 1:-1, 2:] - padded[:, :, 1:-1, :-2]) / 2.0
    return (along_x, along_y, along_z)


def operate(padded_x):
    core = padded_x[:, 1:-1]
    padded = jnp.pad(core, ((0, 0), (0, 0), (1, 1), (1, 1)))
    beside = padded_x[:, 2:] + padded_x[:, :-2]
    beside = beside + padded[:, :, 2:, 1:-1] + padded[:, :, :-2, 1:-1]
    beside = beside + padded[:, :, 1:-1, 2:] + padded[:, :, 1:-1, :-2]
    return 6.0 * core - beside


def search_rims(field):
    return extended(field, (("gx", 1),), 1)


def apply_operator(field):
    return operate(search_rims(field))


def totals(values):
    return jnp.sum(values, axis=(1, 2, 3))


def expand(values):
    return values[:, None, None, None]


def squares(residual):
    return lax.psum(totals(residual * residual), "gx")


def curvature(direction, image):
    return lax.psum(totals(direction * image), "gx")


def per_device(displacement, adjoint, vp_model, vs_model):
    depth = 1
    field_padded = extended(displacement, (("gx", 1),), depth)
    along_x, along_y, along_z = derive(field_padded)
    divergence = along_x[0] + along_y[1] + along_z[2]
    rhs = jnp.stack(
        [-divergence, along_y[2] - along_z[1], along_z[0] - along_x[2], along_x[1] - along_y[0]]
    )
    solution = jnp.zeros_like(rhs)
    residual = rhs
    direction = rhs
    norm_now = squares(residual)
    for iteration in range(ITERS):
        image = apply_operator(direction)
        alpha = norm_now / curvature(direction, image)
        solution = solution + expand(alpha) * direction
        if iteration + 1 < ITERS:
            residual = residual - expand(alpha) * image
            norm_next = squares(residual)
            direction = residual + expand(norm_next / norm_now) * direction
            norm_now = norm_next
    solution_padded = extended(solution, (("gx", 1),), 1)
    along_x, along_y, along_z = derive(solution_padded)
    p_sum = along_x[0] * adjoint[0] + along_y[0] * adjoint[1] + along_z[0] * adjoint[2]
    s_sum = (
        (along_y[3] - along_z[2]) * adjoint[0]
        + (along_z[1] - along_x[3]) * adjoint[1]
        + (along_x[2] - along_y[1]) * adjoint[2]
    )
    return (vp_model * p_sum, vs_model * s_sum)


def solution(mesh):
    in_specs = (
        P(None, ("shots", "gx"), None, None),
        P(None, ("shots", "gx"), None, None),
        P(("shots", "gx"), None, None),
        P(("shots", "gx"), None, None),
    )
    out_specs = (P(("shots", "gx"), None, None), P(("shots", "gx"), None, None))
    return jax.shard_map(
        per_device, mesh=mesh, in_specs=in_specs, out_specs=out_specs, check_vma=False
    )
```

profile of v0, /device:TPU:0, one launch (start us, length us, event | category | flops | bytes accessed | tf_op | source)
XLA Modules:
  0.0 264.9 jit_solution(323750102511292537)
XLA Ops:
  0.6 1.2 fusion.50
  1.8 1.3 collective-permute-start
  3.1 3.1 %collective-permute-start.1 = (f32[3,1,256,128]{3,2,1,0:T(8,128)S(1)}, f32[3,1,256,128]{3,2,1,0:T(8,128)S(1)}, u32[]{:S(2)}, u32[]{:S(2)}) collective-permute-start(f32[3,1,256,128]{3,2,1,0:T(8,128)S(1)} %get-tuple-element.32), channel_id=1, source_target_pairs={{0,1},{1,2},{2,3},{3,4},{4,5},{5,6},{6,7},{7,8},{8,9},{9,10},{10,1... | collective-permute-start | bytes 1179656 | tf_op jit(solution)/shard_map/ppermute | solution.py:14
  6.2 0.0 collective-permute-done
  6.2 1.3 collective-permute-done.1
  7.5 9.1 %fusion.29 = (f32[3,8,256,128]{3,2,1,0:T(8,128)S(1)}, f32[3,8,256,128]{3,2,1,0:T(8,128)S(1)}, f32[3,8,256,128]{3,2,1,0:T(8,128)S(1)}) fusion(f32[3,8,256,128]{3,2,1,0:T(8,128)} %param.4, f32[3,1,256,128]{3,2,1,0:T(8,128)S(1)} %collective-permute-done.1, f32[3,1,256,128]{3,2,1,0:T(8,128)S(1)} %collective-permute-done), kind=kLoop, calls=%fused_computation.74 | loop fusion | flops 6291456 | bytes 13369344 | tf_op jit(solution)/shard_map/div | solution.py:27
  16.6 0.8 fusion.43
  17.4 0.0 copy-start
  17.4 0.5 pad_maximum_fusion.14
  17.9 0.1 fusion.49
  18.0 1.3 collective-permute-start.2
  19.3 11.7 %collective-permute-start.3 = (f32[4,1,256,128]{3,2,1,0:T(8,128)S(1)}, f32[4,1,256,128]{3,2,1,0:T(8,128)S(1)}, u32[]{:S(2)}, u32[]{:S(2)}) collective-permute-start(f32[4,1,256,128]{3,2,1,0:T(8,128)S(1)} %get-tuple-element.27), channel_id=1, source_target_pairs={{0,1},{1,2},{2,3},{3,4},{4,5},{5,6},{6,7},{7,8},{8,9},{9,10},{10,1... | collective-permute-start | bytes 1572872 | tf_op jit(solution)/shard_map/ppermute | solution.py:14
  31.0 0.0 collective-permute-done.2
  31.0 1.5 collective-permute-done.3
  32.5 0.0 copy-done
  32.5 5.7 %multiply_reduce_fusion.3 = (f32[4]{0:T(128)S(1)}, f32[4]{0:T(128)S(1)}, f32[4,8,256,128]{3,2,1,0:T(8,128)}) fusion(f32[1,8,256,128]{3,2,1,0:T(8,128)S(1)} %get-tuple-element.14, f32[1,8,256,128]{3,2,1,0:T(8,128)S(1)} %get-tuple-element.15, f32[1,8,256,128]{3,2,1,0:T(8,128)S(1)} %get-tuple-element.16, f32[1,8,256,128]{3,2,1,0:T(8,128)S(1)} %get-tuple-element.13, ...), kind=kLoop, calls=%fused_computation.68 | loop fusion | flops 23068664 | bytes 13631520 | tf_op jit(solution)/shard_map/reduce_sum | solution.py:49
  38.2 39.8 %all-reduce.5 = (f32[4]{0:T(128)S(1)}, f32[4]{0:T(128)S(1)}) all-reduce(f32[4]{0:T(128)S(1)} %get-tuple-element.3, f32[4]{0:T(128)S(1)} %get-tuple-element.2), channel_id=1, replica_groups=mesh['shots'=2,'gx'=16] {'gx'}, use_global_device_ids=true, to_apply=%region_1.2 | all-reduce | flops 8 | bytes 64 | tf_op jit(solution)/shard_map/psum | solution.py:57
  78.0 4.4 %multiply_reduce_fusion.2 = (f32[4]{0:T(128)S(1)}, f32[4,8,256,128]{3,2,1,0:T(8,128)}) fusion(f32[4,8,256,128]{3,2,1,0:T(8,128)} %get-tuple-element.10, f32[4]{0:T(128)S(1)} %div.36, f32[1,8,256,128]{3,2,1,0:T(8,128)S(1)} %get-tuple-element.14, f32[1,8,256,128]{3,2,1,0:T(8,128)S(1)} %get-tuple-element.15, f32[1,8,256,128]{3,2,1,0:T(8,128)} %copy-done, ...), kind=kLoop, calls=%fused_computation.66 | loop fusion | flops 7340028 | bytes 12582944 | tf_op jit(solution)/shard_map/reduce_sum | solution.py:49
  82.4 29.5 %psum.44 = f32[4]{0:T(128)S(1)} all-reduce(f32[4]{0:T(128)S(1)} %get-tuple-element.8), channel_id=1, replica_groups=mesh['shots'=2,'gx'=16] {'gx'}, use_global_device_ids=true, to_apply=%region_5.6 | all-reduce | flops 4 | bytes 32 | tf_op jit(solution)/shard_map/psum | solution.py:57
  111.9 3.2 %multiply_add_fusion.2 = f32[4,8,256,128]{3,2,1,0:T(8,128)S(1)} fusion(f32[4,8,256,128]{3,2,1,0:T(8,128)} %get-tuple-element.9, f32[4]{0:T(128)S(1)} %div.37, f32[1,8,256,128]{3,2,1,0:T(8,128)S(1)} %get-tuple-element.14, f32[1,8,256,128]{3,2,1,0:T(8,128)S(1)} %get-tuple-element.15, f32[1,8,256,128]{3,2,1,0:T(8,128)} %copy-done, ...), kind=kLoop, calls=%fused_computation.65 | loop fusion | flops 5242880 | bytes 12582928 | tf_op jit(solution)/shard_map/add | solution.py:83
  115.1 0.1 fusion.48
  115.2 1.3 collective-permute-start.4
  116.5 3.1 %collective-permute-start.5 = (f32[4,1,256,128]{3,2,1,0:T(8,128)S(1)}, f32[4,1,256,128]{3,2,1,0:T(8,128)S(1)}, u32[]{:S(2)}, u32[]{:S(2)}) collective-permute-start(f32[4,1,256,128]{3,2,1,0:T(8,128)S(1)} %get-tuple-element.25), channel_id=1, source_target_pairs={{0,1},{1,2},{2,3},{3,4},{4,5},{5,6},{6,7},{7,8},{8,9},{9,10},{10,1... | collective-permute-start | bytes 1572872 | tf_op jit(solution)/shard_map/ppermute | solution.py:14
  119.5 0.0 collective-permute-done.4
  119.5 1.5 collective-permute-done.5
  121.0 4.2 %multiply_reduce_fusion.1 = (f32[4]{0:T(128)S(1)}, f32[4,8,256,128]{3,2,1,0:T(8,128)}) fusion(f32[4,8,256,128]{3,2,1,0:T(8,128)S(1)} %multiply_add_fusion.2, f32[4,1,256,128]{3,2,1,0:T(8,128)S(1)} %collective-permute-done.5, f32[4,1,256,128]{3,2,1,0:T(8,128)S(1)} %collective-permute-done.4), kind=kLoop, calls=%fused_computation.64 | loop fusion | flops 11534332 | bytes 9437200 | tf_op jit(solution)/shard_map/reduce_sum | solution.py:49
  125.2 35.4 %psum.45 = f32[4]{0:T(128)S(1)} all-reduce(f32[4]{0:T(128)S(1)} %get-tuple-element.6), channel_id=1, replica_groups=mesh['shots'=2,'gx'=16] {'gx'}, use_global_device_ids=true, to_apply=%region_7.8 | all-reduce | flops 4 | bytes 32 | tf_op jit(solution)/shard_map/psum | solution.py:61
  160.6 4.3 %multiply_reduce_fusion = f32[4]{0:T(128)S(1)} fusion(f32[4,8,256,128]{3,2,1,0:T(8,128)} %get-tuple-element.9, f32[4,8,256,128]{3,2,1,0:T(8,128)} %get-tuple-element.7, f32[4]{0:T(128)S(1)} %div.38), kind=kLoop, calls=%fused_computation.62 | loop fusion | flops 4194300 | bytes 8388640 | tf_op jit(solution)/shard_map/reduce_sum | solution.py:49
  164.9 29.5 %psum.46 = f32[4]{0:T(128)S(1)} all-reduce(f32[4]{0:T(128)S(1)} %multiply_reduce_fusion), channel_id=1, replica_groups=mesh['shots'=2,'gx'=16] {'gx'}, use_global_device_ids=true, to_apply=%region_9.10 | all-reduce | flops 4 | bytes 32 | tf_op jit(solution)/shard_map/psum | solution.py:57
  194.4 4.3 %multiply_add_fusion.1 = f32[4,8,256,128]{3,2,1,0:T(8,128)S(1)} fusion(f32[4]{0:T(128)S(1)} %div.39, f32[4,8,256,128]{3,2,1,0:T(8,128)} %get-tuple-element.9, f32[4,8,256,128]{3,2,1,0:T(8,128)} %get-tuple-element.7, f32[4]{0:T(128)S(1)} %div.38, f32[1,8,256,128]{3,2,1,0:T(8,128)S(1)} %get-tuple-element.14, f32[1,8,256,128]{3,2,1,0:T(8,128)S(1)} %get-tuple-element.15, ...), kind=kLoop, calls=%fused_computation.61 | loop fusion | flops 9437184 | bytes 16777264 | tf_op jit(solution)/shard_map/add | solution.py:83
  198.7 0.1 fusion.47
  198.7 1.3 collective-permute-start.6
  200.0 3.1 %collective-permute-start.7 = (f32[4,1,256,128]{3,2,1,0:T(8,128)S(1)}, f32[4,1,256,128]{3,2,1,0:T(8,128)S(1)}, u32[]{:S(2)}, u32[]{:S(2)}) collective-permute-start(f32[4,1,256,128]{3,2,1,0:T(8,128)S(1)} %get-tuple-element.23), channel_id=1, source_target_pairs={{0,1},{1,2},{2,3},{3,4},{4,5},{5,6},{6,7},{7,8},{8,9},{9,10},{10,1... | collective-permute-start | bytes 1572872 | tf_op jit(solution)/shard_map/ppermute | solution.py:14
  203.1 0.0 collective-permute-done.6
  203.1 1.5 collective-permute-done.7
  204.6 3.0 %fusion.25 = f32[4]{0:T(128)S(1)} fusion(f32[4,8,256,128]{3,2,1,0:T(8,128)S(1)} %multiply_add_fusion.1, f32[4,1,256,128]{3,2,1,0:T(8,128)S(1)} %collective-permute-done.7, f32[4,1,256,128]{3,2,1,0:T(8,128)S(1)} %collective-permute-done.6), kind=kLoop, calls=%fused_computation.70 | loop fusion | flops 11534332 | bytes 5242896 | tf_op jit(solution)/shard_map/reduce_sum | solution.py:49
  207.6 35.4 %psum.47 = f32[4]{0:T(128)S(1)} all-reduce(f32[4]{0:T(128)S(1)} %fusion.25), channel_id=1, replica_groups=mesh['shots'=2,'gx'=16] {'gx'}, use_global_device_ids=true, to_apply=%region_11.12 | all-reduce | flops 4 | bytes 32 | tf_op jit(solution)/shard_map/psum | solution.py:61
  242.9 4.5 %multiply_add_fusion = f32[4,8,256,128]{3,2,1,0:T(8,128)S(1)} fusion(f32[4]{0:T(128)S(1)} %div.40, f32[4]{0:T(128)S(1)} %div.38, f32[4]{0:T(128)S(1)} %div.36, f32[4]{0:T(128)S(1)} %div.39, f32[4,8,256,128]{3,2,1,0:T(8,128)} %get-tuple-element.9, f32[4,8,256,128]{3,2,1,0:T(8,128)} %get-tuple-element.7, f32[1,8,256,128]{3,2,1,0:T(8,128)S(1)} %get-tuple-element.14, ...), kind=kLoop, calls=%fused_computation.60 | loop fusion | flops 14680064 | bytes 16777296 | tf_op jit(solution)/shard_map/add | solution.py:79
  247.4 0.1 fusion.46
  247.5 1.3 collective-permute-start.8
  248.8 0.0 copy-start.1
  248.8 0.0 copy-start.2
  248.9 0.0 copy-start.3
  248.9 4.1 %collective-permute-start.9 = (f32[4,1,256,128]{3,2,1,0:T(8,128)S(1)}, f32[4,1,256,128]{3,2,1,0:T(8,128)}, u32[]{:S(2)}, u32[]{:S(2)}) collective-permute-start(f32[4,1,256,128]{3,2,1,0:T(8,128)S(1)} %get-tuple-element.21), channel_id=1, source_target_pairs={{0,1},{1,2},{2,3},{3,4},{4,5},{5,6},{6,7},{7,8},{8,9},{9,10},{10,1... | collective-permute-start | bytes 1572872 | tf_op jit(solution)/shard_map/ppermute | solution.py:14
  253.0 0.0 collective-permute-done.8
  253.0 0.0 copy-start.4
  253.0 0.8 copy-done.4
  253.8 0.1 collective-permute-done.9
  253.8 6.4 %fusion.21 = (f32[4,8,256,128]{3,2,1,0:T(8,128)S(1)}, f32[4,8,256,128]{3,2,1,0:T(8,128)S(1)}, f32[4,8,256,128]{3,2,1,0:T(8,128)}) fusion(f32[4,8,256,128]{3,2,1,0:T(8,128)S(1)} %multiply_add_fusion, f32[4,1,256,128]{3,2,1,0:T(8,128)} %collective-permute-done.9, f32[4,1,256,128]{3,2,1,0:T(8,128)} %copy-done.4), kind=kLoop, calls=%fused_computation.42 | loop fusion | flops 8388608 | bytes 17825792 | tf_op jit(solution)/shard_map/div | solution.py:23
  260.2 0.0 copy-done.1
  260.2 0.0 copy-done.2
  260.2 0.0 copy-done.3
  260.2 4.7 %fusion.35 = (f32[8,256,128]{2,1,0:T(8,128)}, f32[8,256,128]{2,1,0:T(8,128)}) fusion(f32[8,256,128]{2,1,0:T(8,128)S(1)} %copy-done.2, f32[4,8,256,128]{3,2,1,0:T(8,128)S(1)} %get-tuple-element.18, f32[4,8,256,128]{3,2,1,0:T(8,128)S(1)} %get-tuple-element.17, f32[4,8,256,128]{3,2,1,0:T(8,128)} %get-tuple-element.19, f32[3,8,256,128]{3,2,1,0:T(8,128)S(1)} %copy-done.1, ...), kind=kLoop, calls=%fused_computation.83 | loop fusion | flops 3932160 | bytes 16777216 | tf_op jit(solution)/shard_map/mul | solution.py:93
  (5 shorter events, 0.0 us)
Async XLA Ops:
  1.8 4.4 %collective-permute-start = (f32[3,1,256,128]{3,2,1,0:T(8,128)S(1)}, f32[3,1,256,128]{3,2,1,0:T(8,128)S(1)}, u32[]{:S(2)}, u32[]{:S(2)}) collective-permute-start(f32[3,1,256,128]{3,2,1,0:T(8,128)S(1)} %get-tuple-element.31), channel_id=1, source_target_pairs={{1,0},{2,1},{3,2},{4,3},{5,4},{6,5},{7,6},{8,7},{9,8},{10,9},{11,1... | collective-permute-start | bytes 1179656 | tf_op jit(solution)/shard_map/ppermute | solution.py:17
  3.1 4.4 %collective-permute-start.1 = (f32[3,1,256,128]{3,2,1,0:T(8,128)S(1)}, f32[3,1,256,128]{3,2,1,0:T(8,128)S(1)}, u32[]{:S(2)}, u32[]{:S(2)}) collective-permute-start(f32[3,1,256,128]{3,2,1,0:T(8,128)S(1)} %get-tuple-element.32), channel_id=1, source_target_pairs={{0,1},{1,2},{2,3},{3,4},{4,5},{5,6},{6,7},{7,8},{8,9},{9,10},{10,1... | collective-permute-start | bytes 1179656 | tf_op jit(solution)/shard_map/ppermute | solution.py:14
  17.4 15.1 %copy-start = (f32[1,8,256,128]{3,2,1,0:T(8,128)}, f32[1,8,256,128]{3,2,1,0:T(8,128)S(1)}, u32[]{:S(2)}) copy-start(f32[1,8,256,128]{3,2,1,0:T(8,128)S(1)} %get-tuple-element.16) | copy-start | bytes 3145732
  18.0 13.0 %collective-permute-start.2 = (f32[4,1,256,128]{3,2,1,0:T(8,128)S(1)}, f32[4,1,256,128]{3,2,1,0:T(8,128)S(1)}, u32[]{:S(2)}, u32[]{:S(2)}) collective-permute-start(f32[4,1,256,128]{3,2,1,0:T(8,128)S(1)} %get-tuple-element.26), channel_id=1, source_target_pairs={{1,0},{2,1},{3,2},{4,3},{5,4},{6,5},{7,6},{8,7},{9,8},{10,9},{11,1... | collective-permute-start | bytes 1572872 | tf_op jit(solution)/shard_map/ppermute | solution.py:17
  19.3 13.2 %collective-permute-start.3 = (f32[4,1,256,128]{3,2,1,0:T(8,128)S(1)}, f32[4,1,256,128]{3,2,1,0:T(8,128)S(1)}, u32[]{:S(2)}, u32[]{:S(2)}) collective-permute-start(f32[4,1,256,128]{3,2,1,0:T(8,128)S(1)} %get-tuple-element.27), channel_id=1, source_target_pairs={{0,1},{1,2},{2,3},{3,4},{4,5},{5,6},{6,7},{7,8},{8,9},{9,10},{10,1... | collective-permute-start | bytes 1572872 | tf_op jit(solution)/shard_map/ppermute | solution.py:14
  115.2 4.4 %collective-permute-start.4 = (f32[4,1,256,128]{3,2,1,0:T(8,128)S(1)}, f32[4,1,256,128]{3,2,1,0:T(8,128)S(1)}, u32[]{:S(2)}, u32[]{:S(2)}) collective-permute-start(f32[4,1,256,128]{3,2,1,0:T(8,128)S(1)} %get-tuple-element.24), channel_id=1, source_target_pairs={{1,0},{2,1},{3,2},{4,3},{5,4},{6,5},{7,6},{8,7},{9,8},{10,9},{11,1... | collective-permute-start | bytes 1572872 | tf_op jit(solution)/shard_map/ppermute | solution.py:17
  116.5 4.6 %collective-permute-start.5 = (f32[4,1,256,128]{3,2,1,0:T(8,128)S(1)}, f32[4,1,256,128]{3,2,1,0:T(8,128)S(1)}, u32[]{:S(2)}, u32[]{:S(2)}) collective-permute-start(f32[4,1,256,128]{3,2,1,0:T(8,128)S(1)} %get-tuple-element.25), channel_id=1, source_target_pairs={{0,1},{1,2},{2,3},{3,4},{4,5},{5,6},{6,7},{7,8},{8,9},{9,10},{10,1... | collective-permute-start | bytes 1572872 | tf_op jit(solution)/shard_map/ppermute | solution.py:14
  198.7 4.4 %collective-permute-start.6 = (f32[4,1,256,128]{3,2,1,0:T(8,128)S(1)}, f32[4,1,256,128]{3,2,1,0:T(8,128)S(1)}, u32[]{:S(2)}, u32[]{:S(2)}) collective-permute-start(f32[4,1,256,128]{3,2,1,0:T(8,128)S(1)} %get-tuple-element.22), channel_id=1, source_target_pairs={{1,0},{2,1},{3,2},{4,3},{5,4},{6,5},{7,6},{8,7},{9,8},{10,9},{11,1... | collective-permute-start | bytes 1572872 | tf_op jit(solution)/shard_map/ppermute | solution.py:17
  200.0 4.6 %collective-permute-start.7 = (f32[4,1,256,128]{3,2,1,0:T(8,128)S(1)}, f32[4,1,256,128]{3,2,1,0:T(8,128)S(1)}, u32[]{:S(2)}, u32[]{:S(2)}) collective-permute-start(f32[4,1,256,128]{3,2,1,0:T(8,128)S(1)} %get-tuple-element.23), channel_id=1, source_target_pairs={{0,1},{1,2},{2,3},{3,4},{4,5},{5,6},{6,7},{7,8},{8,9},{9,10},{10,1... | collective-permute-start | bytes 1572872 | tf_op jit(solution)/shard_map/ppermute | solution.py:14
  247.5 5.4 %collective-permute-start.8 = (f32[4,1,256,128]{3,2,1,0:T(8,128)S(1)}, f32[4,1,256,128]{3,2,1,0:T(8,128)S(1)}, u32[]{:S(2)}, u32[]{:S(2)}) collective-permute-start(f32[4,1,256,128]{3,2,1,0:T(8,128)S(1)} %get-tuple-element.20), channel_id=1, source_target_pairs={{1,0},{2,1},{3,2},{4,3},{5,4},{6,5},{7,6},{8,7},{9,8},{10,9},{11,1... | collective-permute-start | bytes 1572872 | tf_op jit(solution)/shard_map/ppermute | solution.py:17
  248.8 11.4 %copy-start.1 = (f32[3,8,256,128]{3,2,1,0:T(8,128)S(1)}, f32[3,8,256,128]{3,2,1,0:T(8,128)}, u32[]{:S(2)}) copy-start(f32[3,8,256,128]{3,2,1,0:T(8,128)} %param.5) | copy-start | bytes 9437188
  248.8 11.4 %copy-start.2 = (f32[8,256,128]{2,1,0:T(8,128)S(1)}, f32[8,256,128]{2,1,0:T(8,128)}, u32[]{:S(2)}) copy-start(f32[8,256,128]{2,1,0:T(8,128)} %param.7) | copy-start | bytes 3145732
  248.9 11.4 %copy-start.3 = (f32[8,256,128]{2,1,0:T(8,128)S(1)}, f32[8,256,128]{2,1,0:T(8,128)}, u32[]{:S(2)}) copy-start(f32[8,256,128]{2,1,0:T(8,128)} %param.6) | copy-start | bytes 3145732
  248.9 5.0 %collective-permute-start.9 = (f32[4,1,256,128]{3,2,1,0:T(8,128)S(1)}, f32[4,1,256,128]{3,2,1,0:T(8,128)}, u32[]{:S(2)}, u32[]{:S(2)}) collective-permute-start(f32[4,1,256,128]{3,2,1,0:T(8,128)S(1)} %get-tuple-element.21), channel_id=1, source_target_pairs={{0,1},{1,2},{2,3},{3,4},{4,5},{5,6},{6,7},{7,8},{8,9},{9,10},{10,1... | collective-permute-start | bytes 1572872 | tf_op jit(solution)/shard_map/ppermute | solution.py:14
  253.0 0.8 copy-start.4
where the time goes:
time: 269 us; the launch traced here: 265 us
  blocking collectives  169 us (63%)
  other arithmetic  55.1 us (20%)
  starting transfers between devices  31.5 us (12%)
  waiting for transfers between devices  5.8 us (2%)
    psum x3, blocking collectives, squares(): return lax.psum(totals(residual * residual), 'gx')  98.7 us
    psum x2, blocking collectives, curvature(): return lax.psum(totals(direction * image), 'gx')  70.7 us
    ppermute x5, starting transfers between devices, extended(): lax.ppermute(lax.slice_in_dim(block, block.shape[dim] - width, None, axis...  25 us
    reduce_sum x5, other arithmetic, totals(): return jnp.sum(values, axis=(1, 2, 3))  21.6 us
    div x1, other arithmetic, derive(): along_z = (padded[:, :, 1:-1, 2:] - padded[:, :, 1:-1, :-2]) / 2.0  9.12 us
    add x2, other arithmetic, per_device(): direction = residual + expand(norm_next / norm_now) * direction  7.44 us
    ppermute x5, starting transfers between devices, extended(): lax.ppermute(lax.slice_in_dim(block, 0, width, axis=dim), axis, backward)  6.46 us
    div x1, other arithmetic, derive(): along_x = (padded_x[:, 2:] - padded_x[:, :-2]) / 2.0  6.41 us
  transfers between devices with their start and end apart: 10, of which 5 were waited for; matrix products, arithmetic and copies ran while one was open for 0% of the time, Pallas kernels for 0%

commit v1 on v0

v1 whole, which is shorter than its diff:
```python
import functools

import jax
import jax.numpy as jnp
from jax import lax
from jax.experimental import pallas as pl
from jax.experimental.pallas import tpu as pltpu
from jax.sharding import PartitionSpec as P

ITERS = 3
DEPTH = 4
PAD = 8
CHUNK = 32
F32 = jnp.float32
MESH = pl.DeviceIdType.MESH


def kernel(n, nx, ny, nz, u_hbm, adj_hbm, vp_hbm, vs_hbm, kp_hbm, ks_hbm,
           u, basis0, basis1, basis2, parts, adj, vp, vs, out, acc, mom, local_sem,
           send_sem, recv_sem, mom_send, mom_recv, out_sem):
    me = lax.axis_index("gx")
    right, left = lax.rem(me + 1, n), lax.rem(me + n - 1, n)
    has_left, has_right = me > 0, me < n - 1
    bases = (basis0, basis1, basis2)

    loads = [
        pltpu.make_async_copy(u_hbm, u.at[:, pl.ds(DEPTH, nx), pl.ds(PAD, ny)], local_sem.at[0]),
        pltpu.make_async_copy(adj_hbm, adj, local_sem.at[1]),
        pltpu.make_async_copy(vp_hbm, vp, local_sem.at[2]),
        pltpu.make_async_copy(vs_hbm, vs, local_sem.at[3]),
    ]
    loads[0].start()

    barrier = pltpu.get_barrier_semaphore()

    def greet(t, carry):
        pl.semaphore_signal(barrier, inc=1, device_id={"gx": lax.rem(me + t, n)}, device_id_type=MESH)
        return carry

    lax.fori_loop(1, n, greet, 0)
    loads[1].start()

    for ref in (u,) + bases:
        zero = jnp.zeros(ref.shape[:2] + (PAD, nz), F32)
        ref[:, :, pl.ds(0, PAD), :] = zero
        ref[:, :, pl.ds(PAD + ny, PAD), :] = zero
    acc[...] = jnp.zeros_like(acc)

    @pl.when(jnp.logical_not(has_left))
    def _():
        u[:, pl.ds(0, DEPTH)] = jnp.zeros((3, DEPTH) + u.shape[2:], F32)

    @pl.when(jnp.logical_not(has_right))
    def _():
        u[:, pl.ds(DEPTH + nx, DEPTH)] = jnp.zeros((3, DEPTH) + u.shape[2:], F32)

    pl.semaphore_wait(barrier, n - 1)

    rights, lefts = [], []
    for d in range(1, DEPTH + 1):
        rights.append(pltpu.make_async_remote_copy(
            src_ref=u_hbm.at[:, nx - d], dst_ref=u.at[:, DEPTH - d, pl.ds(PAD, ny)],
            send_sem=send_sem.at[0, d - 1], recv_sem=recv_sem.at[0, d - 1],
            device_id={"gx": right}, device_id_type=MESH))
        lefts.append(pltpu.make_async_remote_copy(
            src_ref=u_hbm.at[:, d - 1], dst_ref=u.at[:, DEPTH + nx + d - 1, pl.ds(PAD, ny)],
            send_sem=send_sem.at[1, d - 1], recv_sem=recv_sem.at[1, d - 1],
            device_id={"gx": left}, device_id_type=MESH))

        @pl.when(has_right)
        def _():
            rights[-1].start()

        @pl.when(has_left)
        def _():
            lefts[-1].start()
    loads[2].start()
    loads[3].start()

    lane = lax.broadcasted_iota(jnp.int32, (CHUNK, nz), 1)
    first, last = lane == 0, lane == nz - 1
    inside_left = jnp.where(has_left, 1.0, 0.0).astype(F32)
    inside_right = jnp.where(has_right, 1.0, 0.0).astype(F32)

    def before(value):
        return jnp.where(first, 0.0, pltpu.roll(value, 1, 1))

    def after(value):
        return jnp.where(last, 0.0, pltpu.roll(value, nz - 1, 1))

    def fold(value):
        return jnp.sum(value.reshape(CHUNK // 8, 8, nz), axis=0)

    def shifted(ref, k, p, row, step):
        return ref[k, p, pl.ds(row + step, CHUNK), :]

    def rhs(plane, row, scale):
        def d_x(k):
            return u[k, plane + 1, pl.ds(row, CHUNK), :] - u[k, plane - 1, pl.ds(row, CHUNK), :]

        def d_y(k):
            return shifted(u, k, plane, row, 1) - shifted(u, k, plane, row, -1)

        def d_z(k):
            value = u[k, plane, pl.ds(row, CHUNK), :]
            return after(value) - before(value)

        half = 0.5 if scale is None else 0.5 * scale
        values = (-(d_x(0) + d_y(1) + d_z(2)), d_y(2) - d_z(1), d_z(0) - d_x(2), d_x(1) - d_y(0))
        for k, value in enumerate(values):
            basis0[k, plane - 1, pl.ds(row, CHUNK), :] = value * half

    def stage(j, plane, row, scale, owned):
        source, p = bases[j], plane - 1 - j
        if owned:
            a = [adj[c, plane - DEPTH, pl.ds(row - PAD, CHUNK), :] for c in range(3)]
        sums = []
        for k in range(4):
            mid = source[k, p, pl.ds(row, CHUNK), :]
            xm, xp = source[k, p - 1, pl.ds(row, CHUNK), :], source[k, p + 1, pl.ds(row, CHUNK), :]
            ym, yp = shifted(source, k, p, row, -1), shifted(source, k, p, row, 1)
            zm, zp = before(mid), after(mid)
            image = 6.0 * mid - ((xm + xp) + (ym + yp) + (zm + zp))
            if j < 2:
                bases[j + 1][k, plane - 2 - j, pl.ds(row, CHUNK), :] = image if scale is None else image * scale
            if owned:
                sums.append(fold(mid * mid))
                sums.append(fold(mid * image))
                if k == 0:
                    part = (xp - xm) * a[0] + (yp - ym) * a[1] + (zp - zm) * a[2]
                elif k == 1:
                    part = (zp - zm) * a[1] - (yp - ym) * a[2]
                elif k == 2:
                    part = (xp - xm) * a[2] - (zp - zm) * a[0]
                else:
                    part = (yp - ym) * a[0] - (xp - xm) * a[1]
                parts[j, k, plane - DEPTH, pl.ds(row - PAD, CHUNK), :] = part
        return tuple(sums)

    chunks = ny // CHUNK

    def row_of(c):
        return pl.multiple_of(PAD + c * CHUNK, 8)

    def run_rhs(low, high, scale=None):
        def step(i, carry):
            rhs(low + i // chunks, row_of(i % chunks), scale)
            return carry
        lax.fori_loop(0, (high - low + 1) * chunks, step, 0)

    def run_stage(j, low, high, owned, scale=None):
        zero = jnp.zeros((8, nz), F32)
        def step(i, carry):
            sums = stage(j, low + i // chunks, row_of(i % chunks), scale, owned)
            return tuple(x + y for x, y in zip(carry, sums))
        sums = lax.fori_loop(0, (high - low + 1) * chunks, step, (zero,) * (8 if owned else 0))
        if owned:
            for k in range(4):
                acc[2 * j, k] += sums[2 * k]
                acc[2 * j + 1, k] += sums[2 * k + 1]

    lo, hi = DEPTH, DEPTH + nx - 1
    loads[0].wait()
    run_rhs(lo + 1, hi - 1)
    loads[1].wait()
    run_stage(0, lo + 2, hi - 2, True)
    run_stage(1, lo + 3, hi - 3, True)

    for d in range(1, DEPTH + 1):
        for side in range(2):
            inside = inside_left if side == 0 else inside_right

            @pl.when(has_left if side == 0 else has_right)
            def _():
                (rights if side == 0 else lefts)[d - 1].wait_recv()

            def at(offset):
                return lo + offset - d if side == 0 else hi - offset + d

            run_rhs(at(1), at(1), inside if d > 1 else None)
            for j in range(3):
                plane = at(2 + j)
                owned = d <= 2 + j
                run_stage(j, plane, plane, owned, None if owned else inside)

    rows = lax.broadcasted_iota(jnp.int32, (8, nz), 0)
    lanes = lax.broadcasted_iota(jnp.int32, (8, nz), 1)
    message = jnp.zeros((8, nz), F32)
    for m in range(6):
        tile = jnp.zeros((8, nz), F32)
        for k in range(4):
            tile = jnp.where(rows == k, jnp.sum(acc[m, k], axis=0, keepdims=True), tile)
        message = jnp.where(lanes == m, jnp.sum(tile, axis=1, keepdims=True), message)
    mom[me] = message

    def tell(t, carry):
        there = lax.rem(me + t, n)
        pltpu.make_async_remote_copy(
            src_ref=mom.at[me], dst_ref=mom.at[me], send_sem=mom_send.at[t],
            recv_sem=mom_recv.at[me], device_id={"gx": there}, device_id_type=MESH).start()
        return carry

    def hear(t, carry):
        source = lax.rem(me + t, n)
        pltpu.make_async_remote_copy(
            src_ref=mom.at[me], dst_ref=mom.at[source], send_sem=mom_send.at[t],
            recv_sem=mom_recv.at[source], device_id={"gx": source}, device_id_type=MESH).wait_recv()
        return carry

    lax.fori_loop(1, n, tell, 0)
    lax.fori_loop(1, n, hear, 0)
    total = lax.fori_loop(0, n, lambda t, carry: carry + mom[t], jnp.zeros((8, nz), F32))
    mu = [jnp.broadcast_to(jnp.sum(jnp.where(lanes == m, total, 0.0), axis=1, keepdims=True), (8, nz))
          for m in range(6)]

    def quad(c, shift):
        value = None
        for i in range(len(c)):
            for j in range(i, len(c)):
                term = (c[i] * c[j]) * mu[i + j + shift]
                if i != j:
                    term = term + term
                value = term if value is None else value + term
        return value

    one = jnp.ones((8, nz), F32)
    residual, direction, norm = [one], [one], mu[0]
    coefs = [jnp.zeros((8, nz), F32)] * ITERS
    for iteration in range(ITERS):
        alpha = norm / quad(direction, 1)
        for i, value in enumerate(direction):
            coefs[i] = coefs[i] + alpha * value
        if iteration + 1 < ITERS:
            image = [None] + [alpha * value for value in direction]
            residual = residual + [jnp.zeros((8, nz), F32)]
            residual = [r if v is None else r - v for r, v in zip(residual, image)]
            new = quad(residual, 0)
            beta = new / norm
            direction = [r + beta * v for r, v in zip(residual, direction + [jnp.zeros((8, nz), F32)])]
            norm = new
    weight = [[jnp.broadcast_to(0.5 * coefs[j][k:k + 1, :], (CHUNK, nz)) for k in range(4)] for j in range(3)]

    loads[2].wait()
    loads[3].wait()

    def finish(plane):
        def step(c, carry):
            rows_at = pl.ds(pl.multiple_of(c * CHUNK, 8), CHUNK)
            p_sum = weight[0][0] * parts[0, 0, plane, rows_at, :]
            for j in range(1, 3):
                p_sum = p_sum + weight[j][0] * parts[j, 0, plane, rows_at, :]
            s_sum = None
            for k in range(1, 4):
                for j in range(3):
                    term = weight[j][k] * parts[j, k, plane, rows_at, :]
                    s_sum = term if s_sum is None else s_sum + term
            out[0, plane, rows_at, :] = vp[plane, rows_at, :] * p_sum
            out[1, plane, rows_at, :] = vs[plane, rows_at, :] * s_sum
            return carry
        lax.fori_loop(0, chunks, step, 0)

    stores = []
    for plane in range(nx):
        finish(plane)
        for o, target in enumerate((kp_hbm, ks_hbm)):
            stores.append(pltpu.make_async_copy(out.at[o, plane], target.at[plane], out_sem.at[o, plane]))
            stores[-1].start()

    def sent(t, carry):
        pltpu.make_async_remote_copy(
            src_ref=mom.at[me], dst_ref=mom.at[me], send_sem=mom_send.at[t],
            recv_sem=mom_recv.at[me], device_id={"gx": lax.rem(me + t, n)}, device_id_type=MESH).wait_send()
        return carry

    lax.fori_loop(1, n, sent, 0)
    for d in range(DEPTH):
        @pl.when(has_right)
        def _():
            rights[d].wait_send()

        @pl.when(has_left)
        def _():
            lefts[d].wait_send()
    for store in stores:
        store.wait()


def per_device(displacement, adjoint, vp_model, vs_model):
    n = lax.axis_size("gx")
    _, nx, ny, nz = displacement.shape
    tall = ny + 2 * PAD
    any_space = pl.BlockSpec(memory_space=pl.ANY)
    shape = jax.ShapeDtypeStruct((nx, ny, nz), F32)
    return pl.pallas_call(
        functools.partial(kernel, n, nx, ny, nz),
        out_shape=(shape, shape),
        in_specs=[any_space] * 4,
        out_specs=(any_space, any_space),
        scratch_shapes=[
            pltpu.VMEM((3, nx + 8, tall, nz), F32),
            pltpu.VMEM((4, nx + 6, tall, nz), F32),
            pltpu.VMEM((4, nx + 4, tall, nz), F32),
            pltpu.VMEM((4, nx + 2, tall, nz), F32),
            pltpu.VMEM((3, 4, nx, ny, nz), F32),
            pltpu.VMEM((3, nx, ny, nz), F32),
            pltpu.VMEM((nx, ny, nz), F32),
            pltpu.VMEM((nx, ny, nz), F32),
            pltpu.VMEM((2, nx, ny, nz), F32),
            pltpu.VMEM((6, 4, 8, nz), F32),
            pltpu.VMEM((n, 8, nz), F32),
            pltpu.SemaphoreType.DMA((4,)),
            pltpu.SemaphoreType.DMA((2, DEPTH)),
            pltpu.SemaphoreType.DMA((2, DEPTH)),
            pltpu.SemaphoreType.DMA((n,)),
            pltpu.SemaphoreType.DMA((n,)),
            pltpu.SemaphoreType.DMA((2, nx)),
        ],
        compiler_params=pltpu.CompilerParams(
            collective_id=0, has_side_effects=True, vmem_limit_bytes=56 * 1024 * 1024
        ),
    )(displacement, adjoint, vp_model, vs_model)


def solution(mesh):
    in_specs = (
        P(None, ("shots", "gx"), None, None),
        P(None, ("shots", "gx"), None, None),
        P(("shots", "gx"), None, None),
        P(("shots", "gx"), None, None),
    )
    out_specs = (P(("shots", "gx"), None, None), P(("shots", "gx"), None, None))
    return jax.shard_map(
        per_device, mesh=mesh, in_specs=in_specs, out_specs=out_specs, check_vma=False
    )
```

time: 269 us -> 67.9 us (0.25); the launches traced: 265 us -> 67.8 us
  blocking collectives: 169 us -> 0 us
  Pallas kernels: 0 us -> 62.6 us
  other arithmetic: 55.1 us -> 0 us
  starting transfers between devices: 31.5 us -> 0 us
  waiting for transfers between devices: 5.8 us -> 0 us
    psum x5 -> x0, blocking collectives: 169 us -> none  [the longest x3 98.7 us: squares(): return lax.psum(totals(residual * residual), 'gx')]
    pallas_call x0 -> x1, Pallas kernels: none -> 62.6 us  [per_device(): pl.pallas_call(functools.partial(kernel, n, nx, ny, nz), out_shape=(shape...]
    ppermute x10 -> x0, starting transfers between devices: 31.5 us -> none  [the longest x5 25 us: extended(): lax.ppermute(lax.slice_in_dim(block, block.shape[dim] - width, None, axis...]
    reduce_sum x5 -> x0, other arithmetic: 21.6 us -> none  [totals(): return jnp.sum(values, axis=(1, 2, 3))]
    div x7 -> x0, other arithmetic: 15.6 us -> none  [the longest x1 9.12 us: derive(): along_z = (padded[:, :, 1:-1, 2:] - padded[:, :, 1:-1, :-2]) / 2.0]
    add x3 -> x0, other arithmetic: 11.9 us -> none  [the longest x2 7.44 us: per_device(): direction = residual + expand(norm_next / norm_now) * direction]
    ppermute x10 -> x0, waiting for transfers between devices: 5.8 us -> none  [the longest x5 5.78 us: extended(): lax.ppermute(lax.slice_in_dim(block, block.shape[dim] - width, None, axis...]
    mul x1 -> x0, other arithmetic: 4.69 us -> none  [per_device(): return (vp_model * p_sum, vs_model * s_sum)]
  transfers between devices with their start and end apart: 10 -> 0, of which waited for: 5 -> 0; matrix products, arithmetic and copies ran while one was open for 0% -> 0% of each run, Pallas kernels for 0% -> 0%
where the time goes in v1:
time: 67.9 us; the launch traced here: 67.8 us
  Pallas kernels  62.6 us (92%)
  local copies, waits for them, and re-layouts  4.54 us (7%)
    pallas_call x1, Pallas kernels, per_device(): pl.pallas_call(functools.partial(kernel, n, nx, ny, nz), out_shape=(shape...  62.6 us
    unnamed x2, local copies, waits for them, and re-layouts  4.54 us

profile of v1, /device:TPU:0, one launch (start us, length us, event | category | flops | bytes accessed | tf_op | source)
XLA Modules:
  0.0 67.8 jit_solution(8440898105100171268)
XLA Ops:
  0.6 62.6 %shard_map.59 = (f32[8,256,128]{2,1,0:T(8,128)}, f32[8,256,128]{2,1,0:T(8,128)}) custom-call(f32[3,8,256,128]{3,2,1,0:T(8,128)} %u_hbm.1, f32[3,8,256,128]{3,2,1,0:T(8,128)} %adj_hbm.1, f32[8,256,128]{2,1,0:T(8,128)} %vp_hbm.1, f32[8,256,128]{2,1,0:T(8,128)} %vs_hbm.1), custom_call_target="tpu_custom_call" | custom-call | tf_op jit(solution)/shard_map/pallas_call | solution.py:294
  63.2 2.3 %copy.8 = f32[8,256,128]{2,1,0:T(8,128)} copy(f32[8,256,128]{2,1,0:T(8,128)} %get-tuple-element.4) | data formatting | bytes 2097152
  65.5 2.3 %copy.9 = f32[8,256,128]{2,1,0:T(8,128)} copy(f32[8,256,128]{2,1,0:T(8,128)} %get-tuple-element.5) | data formatting | bytes 2097152

commit v2 on v1

--- a/solution.py
+++ b/solution.py
@@ -10,14 +10,16 @@
 ITERS = 3
 DEPTH = 4
 PAD = 8
-CHUNK = 32
+CHUNK = 256
+WRITE = 64
+SHIFT = 4.0
 F32 = jnp.float32
 MESH = pl.DeviceIdType.MESH
 
 
-def kernel(n, nx, ny, nz, u_hbm, adj_hbm, vp_hbm, vs_hbm, kp_hbm, ks_hbm,
-           u, basis0, basis1, basis2, parts, adj, vp, vs, out, acc, mom, local_sem,
-           send_sem, recv_sem, mom_send, mom_recv, out_sem):
+def kernel(n, nx, ny, nz, u_hbm, adj_hbm, p_out, s_out,
+           u, basis0, basis1, basis2, parts, adj, acc, mom, local_sem,
+           send_sem, recv_sem, mom_send, mom_recv):
     me = lax.axis_index("gx")
     right, left = lax.rem(me + 1, n), lax.rem(me + n - 1, n)
     has_left, has_right = me > 0, me < n - 1
@@ -26,8 +28,6 @@
     loads = [
         pltpu.make_async_copy(u_hbm, u.at[:, pl.ds(DEPTH, nx), pl.ds(PAD, ny)], local_sem.at[0]),
         pltpu.make_async_copy(adj_hbm, adj, local_sem.at[1]),
-        pltpu.make_async_copy(vp_hbm, vp, local_sem.at[2]),
-        pltpu.make_async_copy(vs_hbm, vs, local_sem.at[3]),
     ]
     loads[0].start()
 
@@ -74,8 +74,6 @@
         @pl.when(has_left)
         def _():
             lefts[-1].start()
-    loads[2].start()
-    loads[3].start()
 
     lane = lax.broadcasted_iota(jnp.int32, (CHUNK, nz), 1)
     first, last = lane == 0, lane == nz - 1
@@ -120,7 +118,7 @@
             xm, xp = source[k, p - 1, pl.ds(row, CHUNK), :], source[k, p + 1, pl.ds(row, CHUNK), :]
             ym, yp = shifted(source, k, p, row, -1), shifted(source, k, p, row, 1)
             zm, zp = before(mid), after(mid)
-            image = 6.0 * mid - ((xm + xp) + (ym + yp) + (zm + zp))
+            image = (6.0 - SHIFT) * mid - ((xm + xp) + (ym + yp) + (zm + zp))
             if j < 2:
                 bases[j + 1][k, plane - 2 - j, pl.ds(row, CHUNK), :] = image if scale is None else image * scale
             if owned:
@@ -213,11 +211,13 @@
     mu = [jnp.broadcast_to(jnp.sum(jnp.where(lanes == m, total, 0.0), axis=1, keepdims=True), (8, nz))
           for m in range(6)]
 
-    def quad(c, shift):
+    energy = [SHIFT * mu[m] + mu[m + 1] for m in range(5)]
+
+    def quad(c, sums):
         value = None
         for i in range(len(c)):
             for j in range(i, len(c)):
-                term = (c[i] * c[j]) * mu[i + j + shift]
+                term = (c[i] * c[j]) * sums[i + j]
                 if i != j:
                     term = term + term
                 value = term if value is None else value + term
@@ -227,25 +227,22 @@
     residual, direction, norm = [one], [one], mu[0]
     coefs = [jnp.zeros((8, nz), F32)] * ITERS
     for iteration in range(ITERS):
-        alpha = norm / quad(direction, 1)
+        alpha = norm / quad(direction, energy)
         for i, value in enumerate(direction):
             coefs[i] = coefs[i] + alpha * value
         if iteration + 1 < ITERS:
-            image = [None] + [alpha * value for value in direction]
-            residual = residual + [jnp.zeros((8, nz), F32)]
-            residual = [r if v is None else r - v for r, v in zip(residual, image)]
-            new = quad(residual, 0)
+            none = [jnp.zeros((8, nz), F32)]
+            image = [SHIFT * v + w for v, w in zip(direction + none, none + direction)]
+            residual = [r - alpha * v for r, v in zip(residual + none, image)]
+            new = quad(residual, mu)
             beta = new / norm
-            direction = [r + beta * v for r, v in zip(residual, direction + [jnp.zeros((8, nz), F32)])]
+            direction = [r + beta * v for r, v in zip(residual, direction + none)]
             norm = new
-    weight = [[jnp.broadcast_to(0.5 * coefs[j][k:k + 1, :], (CHUNK, nz)) for k in range(4)] for j in range(3)]
-
-    loads[2].wait()
-    loads[3].wait()
+    weight = [[jnp.broadcast_to(0.5 * coefs[j][k:k + 1, :], (WRITE, nz)) for k in range(4)] for j in range(3)]
 
     def finish(plane):
         def step(c, carry):
-            rows_at = pl.ds(pl.multiple_of(c * CHUNK, 8), CHUNK)
+            rows_at = pl.ds(pl.multiple_of(c * WRITE, 8), WRITE)
             p_sum = weight[0][0] * parts[0, 0, plane, rows_at, :]
             for j in range(1, 3):
                 p_sum = p_sum + weight[j][0] * parts[j, 0, plane, rows_at, :]
@@ -254,17 +251,12 @@
                 for j in range(3):
                     term = weight[j][k] * parts[j, k, plane, rows_at, :]
                     s_sum = term if s_sum is None else s_sum + term
-            out[0, plane, rows_at, :] = vp[plane, rows_at, :] * p_sum
-            out[1, plane, rows_at, :] = vs[plane, rows_at, :] * s_sum
+            p_out[plane, rows_at, :] = p_sum
+            s_out[plane, rows_at, :] = s_sum
             return carry
-        lax.fori_loop(0, chunks, step, 0)
-
-    stores = []
-    for plane in range(nx):
-        finish(plane)
-        for o, target in enumerate((kp_hbm, ks_hbm)):
-            stores.append(pltpu.make_async_copy(out.at[o, plane], target.at[plane], out_sem.at[o, plane]))
-            stores[-1].start()
+        lax.fori_loop(0, ny // WRITE, step, 0)
+
+    lax.fori_loop(0, nx, lambda plane, carry: (finish(plane), carry)[1], 0)
 
     def sent(t, carry):
         pltpu.make_async_remote_copy(
@@ -281,8 +273,6 @@
         @pl.when(has_left)
         def _():
             lefts[d].wait_send()
-    for store in stores:
-        store.wait()
 
 
 def per_device(displacement, adjoint, vp_model, vs_model):
@@ -291,11 +281,11 @@
     tall = ny + 2 * PAD
     any_space = pl.BlockSpec(memory_space=pl.ANY)
     shape = jax.ShapeDtypeStruct((nx, ny, nz), F32)
-    return pl.pallas_call(
+    p_sum, s_sum = pl.pallas_call(
         functools.partial(kernel, n, nx, ny, nz),
         out_shape=(shape, shape),
-        in_specs=[any_space] * 4,
-        out_specs=(any_space, any_space),
+        in_specs=[any_space] * 2,
+        out_specs=(pl.BlockSpec(memory_space=pltpu.VMEM),) * 2,
         scratch_shapes=[
             pltpu.VMEM((3, nx + 8, tall, nz), F32),
             pltpu.VMEM((4, nx + 6, tall, nz), F32),
@@ -303,22 +293,19 @@
             pltpu.VMEM((4, nx + 2, tall, nz), F32),
             pltpu.VMEM((3, 4, nx, ny, nz), F32),
             pltpu.VMEM((3, nx, ny, nz), F32),
-            pltpu.VMEM((nx, ny, nz), F32),
-            pltpu.VMEM((nx, ny, nz), F32),
-            pltpu.VMEM((2, nx, ny, nz), F32),
             pltpu.VMEM((6, 4, 8, nz), F32),
             pltpu.VMEM((n, 8, nz), F32),
-            pltpu.SemaphoreType.DMA((4,)),
+            pltpu.SemaphoreType.DMA((2,)),
             pltpu.SemaphoreType.DMA((2, DEPTH)),
             pltpu.SemaphoreType.DMA((2, DEPTH)),
             pltpu.SemaphoreType.DMA((n,)),
             pltpu.SemaphoreType.DMA((n,)),
-            pltpu.SemaphoreType.DMA((2, nx)),
         ],
         compiler_params=pltpu.CompilerParams(
             collective_id=0, has_side_effects=True, vmem_limit_bytes=56 * 1024 * 1024
         ),
-    )(displacement, adjoint, vp_model, vs_model)
+    )(displacement, adjoint)
+    return vp_model * p_sum, vs_model * s_sum
 
 
 def solution(mesh):

time: 67.9 us -> 55.3 us (0.81)
  Pallas kernels: 62.6 us -> 50.9 us
  local copies, waits for them, and re-layouts: 4.54 us -> 0.01 us
  other arithmetic: 0 us -> 3.52 us
    pallas_call x1, Pallas kernels: 62.6 us -> 50.9 us  [per_device(): pl.pallas_call(functools.partial(kernel, n, nx, ny, nz), out_shape=(shape...]
    unnamed x2 -> x6, local copies, waits for them, and re-layouts: 4.54 us -> 0.01 us
    mul x0 -> x2, other arithmetic: none -> 3.52 us  [per_device(): return (vp_model * p_sum, vs_model * s_sum)]
where the time goes in v2:
time: 55.3 us; the launch traced here: 55.1 us
  Pallas kernels  50.9 us (92%)
  other arithmetic  3.52 us (6%)
  between operations  0.67 us (1%)
    pallas_call x1, Pallas kernels, per_device(): pl.pallas_call(functools.partial(kernel, n, nx, ny, nz), out_shape=(shape...  50.9 us
    mul x2, other arithmetic, per_device(): return (vp_model * p_sum, vs_model * s_sum)  3.52 us

profile of v2, /device:TPU:0, one launch (start us, length us, event | category | flops | bytes accessed | tf_op | source)
XLA Modules:
  0.0 55.1 jit_solution(2997027893017492220)
XLA Ops:
  0.6 0.0 copy-start
  0.6 50.9 %shard_map.59 = (f32[8,256,128]{2,1,0:T(8,128)}, f32[8,256,128]{2,1,0:T(8,128)}) custom-call(f32[3,8,256,128]{3,2,1,0:T(8,128)} %u_hbm.1, f32[3,8,256,128]{3,2,1,0:T(8,128)} %adj_hbm.1), custom_call_target="tpu_custom_call" | custom-call | tf_op jit(solution)/shard_map/pallas_call | solution.py:284
  51.6 0.0 copy-start.1
  51.6 0.0 copy-start.2
  51.6 0.0 copy-done
  51.6 2.4 %mul.6 = f32[8,256,128]{2,1,0:T(8,128)} multiply(f32[8,256,128]{2,1,0:T(8,128)S(1)} %copy-done, f32[8,256,128]{2,1,0:T(8,128)} %get-tuple-element.4) | non-fusion elementwise | flops 262144 | bytes 3145728 | tf_op jit(solution)/shard_map/mul | solution.py:308
  54.0 0.0 copy-done.1
  54.0 0.0 copy-done.2
  54.0 1.1 %mul.7 = f32[8,256,128]{2,1,0:T(8,128)} multiply(f32[8,256,128]{2,1,0:T(8,128)S(1)} %copy-done.1, f32[8,256,128]{2,1,0:T(8,128)S(1)} %copy-done.2) | non-fusion elementwise | flops 262144 | bytes 3145728 | tf_op jit(solution)/shard_map/mul | solution.py:308
Async XLA Ops:
  0.6 50.9 %copy-start = (f32[8,256,128]{2,1,0:T(8,128)S(1)}, f32[8,256,128]{2,1,0:T(8,128)}, u32[]{:S(2)}) copy-start(f32[8,256,128]{2,1,0:T(8,128)} %param.6) | copy-start | bytes 3145732
  51.6 2.5 %copy-start.1 = (f32[8,256,128]{2,1,0:T(8,128)S(1)}, f32[8,256,128]{2,1,0:T(8,128)}, u32[]{:S(2)}) copy-start(f32[8,256,128]{2,1,0:T(8,128)} %param.7) | copy-start | bytes 3145732
  51.6 2.5 %copy-start.2 = (f32[8,256,128]{2,1,0:T(8,128)S(1)}, f32[8,256,128]{2,1,0:T(8,128)}, u32[]{:S(2)}) copy-start(f32[8,256,128]{2,1,0:T(8,128)} %get-tuple-element.5) | copy-start | bytes 3145732
